TPU v7x, 32 devices: a whole 2x2x4 slice. The times are simulated.
32 devices in a mesh: tm: 8 (over z, x), row: 4 (over y, core).
Axes of the slice: x: 2, y: 2, z: 4, core: 2. Of those that a mesh axis runs over, the one named last changes fastest.
Arguments:
- inputs: bfloat16 [1, 512, 16, 16, 256], P(None, 'tm', 'row'), may hold values from -6 to 6
- decays: float32 [512, 256], P('tm'), may hold values from 0.4 to 0.999999, as said below
- in_kernel: bfloat16 [3, 3, 256, 256], replicated, may hold values from -0.125 to 0.125
- out_kernel: bfloat16 [3, 3, 256, 256], replicated, may hold values from -0.125 to 0.125
- skip: float32 [256], replicated, may hold values from -1 to 1
- cotangent: bfloat16 [1, 512, 16, 16, 256], P(None, 'tm', 'row'), may hold values from -6 to 6
Outputs:
- outputs: bfloat16 [1, 512, 16, 16, 256], P(None, 'tm', 'row')
- in_kernel_grad: float32 [3, 3, 256, 256], replicated
- out_kernel_grad: float32 [3, 3, 256, 256], replicated
Inputs may be any that keep to these rules, and one draw needn't show every extreme that they name: `decays`: strictly below one.
All inputs are finite; a program needn't handle non-finite values.
Results may differ from a plain program's by a relative error of at most 0.0043.
Values may be sent and summed in bfloat16 or wider, within the bound.
No kernel may reach another device: no remote copies, remote signals or barrier semaphores. Data moves between devices by JAX's collectives and lax.ppermute only.
A program may use at most 128 MiB of HBM per device.

v0:
```python
import functools
import math

import jax
import jax.numpy as jnp
from jax import lax
from jax.experimental import pallas as pl
from jax.experimental.pallas import tpu as pltpu
from jax.sharding import PartitionSpec as P

BF16 = jnp.bfloat16
F32 = jnp.float32


def params(mib=44):
    return pltpu.CompilerParams(
        dimension_semantics=("arbitrary",), vmem_limit_bytes=mib * 1024 * 1024
    )


def cost(flops, nbytes):
    return pl.CostEstimate(flops=int(flops), bytes_accessed=int(nbytes), transcendentals=0)


def shifted(cells, width):
    count = cells.shape[0]
    wide = cells.astype(F32)
    column = lax.broadcasted_iota(jnp.int32, (count, 1), 0) % width
    left = jnp.where(column == 0, 0.0, pltpu.roll(wide, 1, 0))
    right = jnp.where(column == width - 1, 0.0, pltpu.roll(wide, count - 1, 0))
    return jnp.concatenate([left.astype(BF16), cells, right.astype(BF16)], axis=1)


def flat(block):
    return block.reshape(-1, block.shape[-1])


def dot(a, b):
    return jnp.dot(a, b, preferred_element_type=F32)


def interior_body(x_ref, w_ref, out_ref, s_ref):
    frames, rows, width, _ = x_ref.shape
    lines = frames * width
    for r in range(rows):
        s_ref[r] = shifted(flat(x_ref[:, r]), width)

    def conv(first, count, taps):
        lhs = jnp.concatenate(
            [flat(s_ref[first + i - 1 : first + i - 1 + count]) for i in taps], axis=1
        )
        rhs = w_ref[taps[0] : taps[-1] + 1].reshape(len(taps) * w_ref.shape[1], w_ref.shape[2])
        out_ref[first : first + count] = dot(lhs, rhs).reshape(count, frames, width, -1)

    conv(1, rows - 2, (0, 1, 2))
    conv(0, 1, (1, 2))
    conv(rows - 1, 1, (0, 1))


def interior_plain_kernel(x_ref, w_ref, out_ref, s_ref):
    interior_body(x_ref, w_ref, out_ref, s_ref)


def interior_flipped_kernel(x_ref, w_ref, out_ref, wt_ref, s_ref):
    @pl.when(pl.program_id(0) == 0)
    def _():
        for i in range(3):
            for j in range(3):
                c = w_ref.shape[3]
                wt_ref[i, j * c : (j + 1) * c, :] = w_ref[2 - i, 2 - j].T

    interior_body(x_ref, wt_ref, out_ref, s_ref)


def interior_conv(x, w, flipped, block):
    frames, rows, width, c = x.shape
    p = w.shape[2] if flipped else w.shape[3]
    part_shape = jax.ShapeDtypeStruct((rows, frames, width, p), F32)
    part_spec = pl.BlockSpec((rows, block, width, p), lambda b: (0, b, 0, 0))
    x_spec = pl.BlockSpec((block, rows, width, c), lambda b: (b, 0, 0, 0))
    scratch = [pltpu.VMEM((rows, block * width, 3 * c), BF16)]
    estimate = cost(2 * frames * rows * width * 9 * c * p, 8 * 2**20)
    taps_spec = pl.BlockSpec((3, 3 * c, p), lambda b: (0, 0, 0))
    if flipped:
        return pl.pallas_call(
            interior_flipped_kernel,
            grid=(frames // block,),
            in_specs=[x_spec, pl.BlockSpec(w.shape, lambda b: (0, 0, 0, 0))],
            out_specs=[part_spec, taps_spec],
            out_shape=[part_shape, jax.ShapeDtypeStruct((3, 3 * c, p), BF16)],
            scratch_shapes=scratch,
            compiler_params=params(),
            cost_estimate=estimate,
            name="interior_cot",
        )(x, w)
    taps = w.reshape(3, 3 * c, p)
    part = pl.pallas_call(
        interior_plain_kernel,
        grid=(frames // block,),
        in_specs=[x_spec, taps_spec],
        out_specs=part_spec,
        out_shape=part_shape,
        scratch_shapes=scratch,
        compiler_params=params(),
        cost_estimate=estimate,
        name="interior_in",
    )(x, taps)
    return part, taps


def scan_kernel(backward, part_ref, up_ref, down_ref, w_ref, decay_ref, local_ref, product_ref, end_ref, carry_ref, run_ref):
    rows, frames, width, p = part_ref.shape
    lines = rows * width

    @pl.when(pl.program_id(0) == 0)
    def _():
        carry_ref[...] = jnp.zeros_like(carry_ref)
        run_ref[...] = jnp.ones_like(run_ref)

    top = dot(shifted(flat(up_ref[...]), width), w_ref[0]).reshape(frames, width, p)
    low = dot(shifted(flat(down_ref[...]), width), w_ref[2]).reshape(frames, width, p)
    decay = decay_ref[...]
    scale = jnp.sqrt((1.0 - decay) * (1.0 + decay))
    state = [carry_ref[r * width : (r + 1) * width] for r in range(rows)]
    run = run_ref[0:1]
    for step in range(frames):
        t = frames - 1 - step if backward else step
        factor = decay[t : t + 1]
        gain = scale[t : t + 1]
        if backward:
            product_ref[t : t + 1] = run
        run = run * factor
        if not backward:
            product_ref[t : t + 1] = run
        for r in range(rows):
            term = part_ref[r, t]
            if r == 0:
                term = term + top[t]
            if r == rows - 1:
                term = term + low[t]
            if backward:
                full = term + state[r]
                local_ref[r, t] = full
                state[r] = factor * full
            else:
                state[r] = factor * state[r] + gain * term
                local_ref[r, t] = state[r]
    for r in range(rows):
        carry_ref[r * width : (r + 1) * width] = state[r]
        end_ref[r * width : (r + 1) * width] = state[r]
    run_ref[...] = jnp.broadcast_to(run, run_ref.shape)
    end_ref[lines : lines + 8] = jnp.broadcast_to(run, (8, p))


def local_scan(part, up, down, taps, decays, backward, block):
    rows, frames, width, p = part.shape
    c = up.shape[-1]
    blocks = frames // block
    at = (lambda b: blocks - 1 - b) if backward else (lambda b: b)
    halo_spec = pl.BlockSpec((block, width, c), lambda b: (at(b), 0, 0))
    part_spec = pl.BlockSpec((rows, block, width, p), lambda b: (0, at(b), 0, 0))
    frame_spec = pl.BlockSpec((block, p), lambda b: (at(b), 0))
    lines = rows * width + 8
    return pl.pallas_call(
        functools.partial(scan_kernel, backward),
        grid=(blocks,),
        in_specs=[
            part_spec,
            halo_spec,
            halo_spec,
            pl.BlockSpec(taps.shape, lambda b: (0, 0, 0)),
            frame_spec,
        ],
        out_specs=[part_spec, frame_spec, pl.BlockSpec((lines, p), lambda b: (0, 0))],
        out_shape=[
            jax.ShapeDtypeStruct(part.shape, F32),
            jax.ShapeDtypeStruct((frames, p), F32),
            jax.ShapeDtypeStruct((lines, p), F32),
        ],
        scratch_shapes=[pltpu.VMEM((rows * width, p), F32), pltpu.VMEM((8, p), F32)],
        compiler_params=params(),
        cost_estimate=cost(4 * frames * width * 3 * c * p, 12 * 2**20),
        name="scan_back" if backward else "scan_fwd",
    )(part, up, down, taps, decays)


def combine(place_ref, ends_ref, total_ref, backward):
    place = place_ref[0]
    count = ends_ref.shape[0]
    lines = total_ref.shape[0]
    total = jnp.zeros(total_ref.shape, F32)
    order = range(count - 1, -1, -1) if backward else range(count)
    for k in order:
        passed = ends_ref[k, lines : lines + 1] * total + ends_ref[k, 0:lines]
        total = jnp.where(k > place if backward else k < place, passed, total)
    total_ref[...] = total


def fill_rim(s_ref, up_ref, x_ref, down_ref):
    _, rows, width, _ = x_ref.shape
    s_ref[0] = shifted(flat(up_ref[...]), width)
    for r in range(rows):
        s_ref[r + 1] = shifted(flat(x_ref[:, r]), width)
    s_ref[rows + 1] = shifted(flat(down_ref[...]), width)


def out_grad_kernel(place_ref, ends_ref, local_ref, product_ref, cot_ref, up_ref, down_ref, low_ref, grad_ref, s_ref, total_ref):
    rows, frames, width, p = local_ref.shape
    c = cot_ref.shape[-1]

    @pl.when(pl.program_id(0) == 0)
    def _():
        combine(place_ref, ends_ref, total_ref, False)
        grad_ref[...] = jnp.zeros_like(grad_ref)

    fill_rim(s_ref, up_ref, cot_ref, down_ref)
    product = product_ref[...]
    turned = []
    for r in range(rows):
        state = local_ref[r] + product[:, None, :] * total_ref[r * width : (r + 1) * width][None]
        low = state.astype(BF16)
        low_ref[r] = low
        turned.append(flat(low).T)
    turned = jnp.concatenate(turned, axis=1)
    for i in range(3):
        gain = dot(turned, flat(s_ref[2 - i : 2 - i + rows]))
        for j in range(3):
            grad_ref[3 * i + j] += gain[:, (2 - j) * c : (3 - j) * c]


def in_grad_kernel(place_ref, ends_ref, local_ref, product_ref, decay_ref, x_ref, up_ref, down_ref, grad_ref, s_ref, total_ref, sum_ref):
    rows, frames, width, p = local_ref.shape
    c = x_ref.shape[-1]

    @pl.when(pl.program_id(0) == 0)
    def _():
        combine(place_ref, ends_ref, total_ref, True)
        sum_ref[...] = jnp.zeros_like(sum_ref)

    fill_rim(s_ref, up_ref, x_ref, down_ref)
    product = product_ref[...]
    decay = decay_ref[...]
    scale = jnp.sqrt((1.0 - decay) * (1.0 + decay))[:, None, :]
    turned = []
    for r in range(rows):
        adjoint = local_ref[r] + product[:, None, :] * total_ref[r * width : (r + 1) * width][None]
        turned.append(flat((scale * adjoint).astype(BF16)).T)
    turned = jnp.concatenate(turned, axis=1)
    for i in range(3):
        sum_ref[i] += dot(turned, flat(s_ref[i : i + rows]))

    @pl.when(pl.program_id(0) == pl.num_programs(0) - 1)
    def _():
        for i in range(3):
            for j in range(3):
                grad_ref[3 * i + j] = sum_ref[i, :, j * c : (j + 1) * c].T


def kernel_grads(place, ends, local, product, x, up, down, decays, block):
    rows, frames, width, p = local.shape
    c = x.shape[-1]
    halo_spec = pl.BlockSpec((block, width, c), lambda b: (b, 0, 0))
    local_spec = pl.BlockSpec((rows, block, width, p), lambda b: (0, b, 0, 0))
    frame_spec = pl.BlockSpec((block, p), lambda b: (b, 0))
    x_spec = pl.BlockSpec((block, rows, width, c), lambda b: (b, 0, 0, 0))
    lead = [
        pl.BlockSpec(memory_space=pltpu.SMEM),
        pl.BlockSpec(ends.shape, lambda b: (0, 0, 0)),
        local_spec,
        frame_spec,
    ]
    tail = [x_spec, halo_spec, halo_spec]
    scratch = [
        pltpu.VMEM((rows + 2, block * width, 3 * c), BF16),
        pltpu.VMEM((rows * width, p), F32),
    ]
    estimate = cost(2 * frames * rows * width * 9 * c * p, 10 * 2**20)
    if decays is None:
        return pl.pallas_call(
            out_grad_kernel,
            grid=(frames // block,),
            in_specs=lead + tail,
            out_specs=[local_spec, pl.BlockSpec((9, p, c), lambda b: (0, 0, 0))],
            out_shape=[
                jax.ShapeDtypeStruct(local.shape, BF16),
                jax.ShapeDtypeStruct((9, p, c), F32),
            ],
            scratch_shapes=scratch,
            compiler_params=params(),
            cost_estimate=estimate,
            name="out_grad",
        )(place, ends, local, product, x, up, down)
    return pl.pallas_call(
        in_grad_kernel,
        grid=(frames // block,),
        in_specs=lead + [frame_spec] + tail,
        out_specs=pl.BlockSpec((9, c, p), lambda b: (0, 0, 0)),
        out_shape=jax.ShapeDtypeStruct((9, c, p), F32),
        scratch_shapes=scratch + [pltpu.VMEM((3, p, 3 * c), F32)],
        compiler_params=params(),
        cost_estimate=estimate,
        name="in_grad",
    )(place, ends, local, product, decays, x, up, down)


def outputs_kernel(low_ref, up_ref, down_ref, w_ref, x_ref, skip_ref, out_ref, s_ref):
    rows, frames, width, p = low_ref.shape
    s_ref[0] = shifted(flat(up_ref[...]), width)
    for r in range(rows):
        s_ref[r + 1] = shifted(flat(low_ref[r]), width)
    s_ref[rows + 1] = shifted(flat(down_ref[...]), width)
    lhs = jnp.concatenate([flat(s_ref[i : i + rows]) for i in range(3)], axis=1)
    mixed = dot(lhs, flat(w_ref[...])).reshape(rows, frames, width, -1)
    skip = skip_ref[...][0:1].reshape(1, 1, -1)
    for r in range(rows):
        out_ref[:, r] = (mixed[r] + skip * x_ref[:, r].astype(F32)).astype(BF16)


def outputs_conv(low, up, down, taps, x, skip, block):
    rows, frames, width, p = low.shape
    c = x.shape[-1]
    halo_spec = pl.BlockSpec((block, width, p), lambda b: (b, 0, 0))
    x_spec = pl.BlockSpec((block, rows, width, c), lambda b: (b, 0, 0, 0))
    return pl.pallas_call(
        outputs_kernel,
        grid=(frames // block,),
        in_specs=[
            pl.BlockSpec((rows, block, width, p), lambda b: (0, b, 0, 0)),
            halo_spec,
            halo_spec,
            pl.BlockSpec(taps.shape, lambda b: (0, 0, 0)),
            x_spec,
            pl.BlockSpec((1, c), lambda b: (0, 0)),
        ],
        out_specs=x_spec,
        out_shape=jax.ShapeDtypeStruct(x.shape, BF16),
        scratch_shapes=[pltpu.VMEM((rows + 2, block * width, 3 * p), BF16)],
        compiler_params=params(),
        cost_estimate=cost(2 * frames * rows * width * 9 * c * p, 8 * 2**20),
        name="outputs_conv",
    )(low, up, down, taps, x, skip)


def row_halo(first, last):
    count = lax.axis_size("row")
    up = lax.ppermute(last, "row", [(i, i + 1) for i in range(count - 1)])
    down = lax.ppermute(first, "row", [(i + 1, i) for i in range(count - 1)])
    return up, down


def reduced_share(grad, scale):
    place = lax.axis_index("row")
    bit = 1
    while bit < lax.axis_size("row"):
        half = grad.shape[0] // 2
        side = (place // bit) % 2
        sent = lax.dynamic_slice_in_dim(grad, (1 - side) * half, half, 0).astype(BF16)
        kept = lax.dynamic_slice_in_dim(grad, side * half, half, 0)
        pairs = [(i, i ^ bit) for i in range(lax.axis_size("row"))]
        grad = kept + lax.ppermute(sent, "row", pairs).astype(F32)
        bit *= 2
    count = lax.axis_size("tm")
    parts = grad.astype(BF16).reshape(count, grad.shape[0] // count, grad.shape[1])
    parts = lax.all_to_all(parts, "tm", 0, 0)
    return (jnp.sum(parts.astype(F32), axis=0) * scale).astype(BF16)


def gathered(share):
    whole = lax.all_gather(share, "tm", axis=0, tiled=True)
    place = lax.axis_index("row")
    bit = lax.axis_size("row") // 2
    while bit >= 1:
        side = (place // bit) % 2
        pairs = [(i, i ^ bit) for i in range(lax.axis_size("row"))]
        other = lax.ppermute(whole, "row", pairs)
        whole = jnp.where(
            side == 0,
            jnp.concatenate([whole, other], axis=0),
            jnp.concatenate([other, whole], axis=0),
        )
        bit //= 2
    return whole.astype(F32)


def per_device(inputs, decays, in_kernel, out_kernel, skip, cotangent):
    clips, frames, rows, width, c = inputs.shape
    p = in_kernel.shape[3]
    block = 16
    grad_scale = 1.0 / math.sqrt(
        clips * frames * lax.axis_size("tm") * rows * lax.axis_size("row") * width
    )
    x = inputs.reshape(frames, rows, width, c)
    cot = cotangent.reshape(frames, rows, width, c)
    place = lax.axis_index("tm").astype(jnp.int32).reshape(1)

    cot_up, cot_down = row_halo(cot[:, 0], cot[:, rows - 1])
    x_up, x_down = row_halo(x[:, 0], x[:, rows - 1])

    cot_part, cot_taps = interior_conv(cot, out_kernel, True, block)
    x_part, x_taps = interior_conv(x, in_kernel, False, block)

    states, running, ends = local_scan(x_part, x_up, x_down, x_taps, decays, False, block)
    all_ends = lax.all_gather(ends, "tm")
    adjoint, trailing, starts = local_scan(
        cot_part, cot_up, cot_down, cot_taps, decays, True, block
    )
    all_starts = lax.all_gather(starts, "tm")

    low, out_grad = kernel_grads(
        place, all_ends, states, running, cot, cot_up, cot_down, None, block
    )
    low_up, low_down = row_halo(low[0], low[rows - 1])
    out_share = reduced_share(out_grad.reshape(-1, c), grad_scale)
    in_grad = kernel_grads(
        place, all_starts, adjoint, trailing, x, x_up, x_down, decays, block
    )
    in_share = reduced_share(in_grad.reshape(-1, p), grad_scale)

    outputs = outputs_conv(
        low, low_up, low_down, out_kernel.reshape(3, 3 * p, c), x, skip.reshape(1, c), block
    )
    return (
        outputs.reshape(inputs.shape),
        gathered(in_share).reshape(in_kernel.shape),
        gathered(out_share).reshape(out_kernel.shape),
    )


def solution(mesh):
    return jax.shard_map(
        per_device,
        mesh=mesh,
        in_specs=(
            P(None, "tm", "row", None, None),
            P("tm", None),
            P(),
            P(),
            P(),
            P(None, "tm", "row", None, None),
        ),
        out_specs=(P(None, "tm", "row", None, None), P(), P()),
        check_vma=False,
    )
```

profile of v0, /device:TPU:1, one launch (start us, length us, event | category | flops | bytes accessed | tf_op | source)
XLA Modules:
  0.0 253.4 jit_solution(17650545347861587373)
XLA Ops:
  3.5 4.5 %collective-permute-start = (bf16[64,16,256]{2,1,0:T(8,128)(2,1)}, bf16[64,16,256]{2,1,0:T(8,128)(2,1)}, u32[]{:S(2)}, u32[]{:S(2)}) collective-permute-start(bf16[64,16,256]{2,1,0:T(8,128)(2,1)} %get-tuple-element.28), channel_id=1, source_target_pairs={{0,1},{1,2},{2,3},{4,5},{5,6},{6,7},{8,9},{9,10},{10,11},{12,13},{... | collective-permute-start | bytes 1572872 | tf_op jit(solution)/shard_map/ppermute | solution.py:346
  11.2 3.8 %collective-permute-start.2 = (bf16[64,16,256]{2,1,0:T(8,128)(2,1)}, bf16[64,16,256]{2,1,0:T(8,128)(2,1)}, u32[]{:S(2)}, u32[]{:S(2)}) collective-permute-start(bf16[64,16,256]{2,1,0:T(8,128)(2,1)} %get-tuple-element.26), channel_id=1, source_target_pairs={{0,1},{1,2},{2,3},{4,5},{5,6},{6,7},{8,9},{9,10},{10,11},{12,13},{... | collective-permute-start | bytes 1572872 | tf_op jit(solution)/shard_map/ppermute | solution.py:346
  16.9 5.1 %interior_in.1.part_ref = f32[4,64,16,256]{3,2,1,0:T(8,128)S(1)} custom-call(bf16[64,4,16,256]{3,2,1,0:T(8,128)(2,1)S(1)} %bitcast.37, bf16[3,768,256]{2,1,0:T(8,128)(2,1)S(1)} %bitcast.44), custom_call_target="tpu_custom_call" | custom-call | flops 4831838208 | bytes 8388608 | tf_op jit(solution)/shard_map/interior_in/pallas_call | solution.py:97
  24.0 5.4 %interior_cot.1 = (f32[4,64,16,256]{3,2,1,0:T(8,128)S(1)}, bf16[3,768,256]{2,1,0:T(8,128)(2,1)S(1)}) custom-call(bf16[64,4,16,256]{3,2,1,0:T(8,128)(2,1)S(1)} %bitcast.35, bf16[3,3,256,256]{3,2,1,0:T(8,128)(2,1)S(1)} %copy-done.14), custom_call_target="tpu_custom_call" | custom-call | flops 4831838208 | bytes 8388608 | tf_op jit(solution)/shard_map/interior_cot/pallas_call | solution.py:85
  29.4 2.0 copy-done
  32.5 4.2 %scan_fwd.1 = (f32[4,64,16,256]{3,2,1,0:T(8,128)S(1)}, f32[64,256]{1,0:T(8,128)S(1)}, f32[72,256]{1,0:T(8,128)S(1)}) custom-call(f32[4,64,16,256]{3,2,1,0:T(8,128)} %copy-done.1, bf16[64,16,256]{2,1,0:T(8,128)(2,1)} %collective-permute-done.up_ref, bf16[64,16,256]{2,1,0:T(8,128)(2,1)} %collective-permute-done.1.down_ref, bf16[3,768,256]{2,1,0:T(8,128)(2,1)S(1)} %bitcast.45, ...), custom_call_target="tpu_custom_call" | custom-call | flops 805306368 | bytes 12582912 | tf_op jit(solution)/shard_map/scan_fwd/pallas_call | solution.py:164
  38.6 26.2 %all-gather = f32[576,256]{1,0:T(8,128)S(1)} all-gather(f32[72,256]{1,0:T(8,128)S(1)} %get-tuple-element.13), channel_id=2, replica_groups=mesh['tm'=8,'row'=4] {'tm'}, dimensions={0}, use_global_device_ids=true | all-gather | bytes 663552 | tf_op jit(solution)/shard_map/all_gather | solution.py:403
  64.8 4.5 %scan_back.1 = (f32[4,64,16,256]{3,2,1,0:T(8,128)S(1)}, f32[64,256]{1,0:T(8,128)S(1)}, f32[72,256]{1,0:T(8,128)S(1)}) custom-call(f32[4,64,16,256]{3,2,1,0:T(8,128)} %copy-done, bf16[64,16,256]{2,1,0:T(8,128)(2,1)} %collective-permute-done.2.up_ref, bf16[64,16,256]{2,1,0:T(8,128)(2,1)} %collective-permute-done.3.down_ref, ...), custom_call_target="tpu_custom_call" | custom-call | flops 805306368 | bytes 12582912 | tf_op jit(solution)/shard_map/scan_back/pallas_call | solution.py:164
  69.3 2.0 copy-done.13
  71.4 25.7 %all-gather.1 = f32[576,256]{1,0:T(8,128)S(1)} all-gather(f32[72,256]{1,0:T(8,128)S(1)} %get-tuple-element.19), channel_id=3, replica_groups=mesh['tm'=8,'row'=4] {'tm'}, dimensions={0}, use_global_device_ids=true | all-gather | bytes 663552 | tf_op jit(solution)/shard_map/all_gather | solution.py:407
  97.1 8.8 %in_grad.1 = f32[9,256,256]{2,1,0:T(8,128)S(1)} custom-call(s32[1]{0:T(128)} %bitcast.place_ref, f32[8,72,256]{2,1,0:T(8,128)S(1)} %bitcast.47, f32[4,64,16,256]{3,2,1,0:T(8,128)} %copy-done.13, f32[64,256]{1,0:T(8,128)S(1)} %get-tuple-element.21.product_ref, f32[64,256]{1,0:T(8,128)S(1)} %copy-done.11, bf16[64,4,16,256]{3,2,1,0:T(8,128)(2,1)S(1)} %bitcast.38, ...), custom_call_target="tpu_custom_call" | custom-call | flops 4831838208 | bytes 10485760 | tf_op jit(solution)/shard_map/in_grad/pallas_call | solution.py:293
  106.0 10.3 %collective-permute-start.6 = (bf16[1152,256]{1,0:T(8,128)(2,1)S(1)}, bf16[1152,256]{1,0:T(8,128)(2,1)S(1)}, u32[]{:S(2)}, u32[]{:S(2)}) collective-permute-start(bf16[1152,256]{1,0:T(8,128)(2,1)S(1)} %dynamic-slice_convert_fusion.1), channel_id=1, source_target_pairs={{0,1},{1,0},{2,3},{3,2},{4,5},{5,4},{6,7},{7,6},{8,9},{9,8},{10,11... | collective-permute-start | bytes 1769480 | tf_op jit(solution)/shard_map/ppermute | solution.py:360
  116.3 8.3 %out_grad.1 = (bf16[4,64,16,256]{3,2,1,0:T(8,128)(2,1)S(1)}, f32[9,256,256]{2,1,0:T(8,128)S(1)}) custom-call(s32[1]{0:T(128)} %bitcast.place_ref, f32[8,72,256]{2,1,0:T(8,128)S(1)} %bitcast.46, f32[4,64,16,256]{3,2,1,0:T(8,128)} %copy-done.12, f32[64,256]{1,0:T(8,128)S(1)} %get-tuple-element.15.product_ref, bf16[64,4,16,256]{3,2,1,0:T(8,128)(2,1)S(1)} %bitcast.36, ...), custom_call_target="tpu_custom_call" | custom-call | flops 4831838208 | bytes 10485760 | tf_op jit(solution)/shard_map/out_grad/pallas_call | solution.py:279
  126.0 3.1 %collective-permute-start.7 = (bf16[576,256]{1,0:T(8,128)(2,1)S(1)}, bf16[576,256]{1,0:T(8,128)(2,1)S(1)}, u32[]{:S(2)}, u32[]{:S(2)}) collective-permute-start(bf16[576,256]{1,0:T(8,128)(2,1)S(1)} %dynamic-slice_convert_fusion.3), channel_id=1, source_target_pairs={{0,2},{1,3},{2,0},{3,1},{4,6},{5,7},{6,4},{7,5},{8,10},{9,11},{10,... | collective-permute-start | bytes 884744 | tf_op jit(solution)/shard_map/ppermute | solution.py:360
  130.1 6.4 %collective-permute-done.7 = bf16[576,256]{1,0:T(8,128)(2,1)S(1)} collective-permute-done((bf16[576,256]{1,0:T(8,128)(2,1)S(1)}, bf16[576,256]{1,0:T(8,128)(2,1)S(1)}, u32[]{:S(2)}, u32[]{:S(2)}) %collective-permute-start.7) | collective-permute-done | bytes 294944 | tf_op jit(solution)/shard_map/ppermute | solution.py:360
  137.2 5.3 %all-to-all-start = ((bf16[8,72,256]{2,1,0:T(8,128)(2,1)}), bf16[8,72,256]{2,1,0:T(8,128)(2,1)S(1)}, u32[]{:S(2)}, u32[]{:S(2)}) async-start(bf16[8,72,256]{2,1,0:T(8,128)(2,1)} %bitcast.18), calls=%async_computation | async-start | bytes 589824 | tf_op jit(solution)/shard_map/all_to_all | solution.py:364
  143.6 6.6 %all-to-all-done = bf16[8,72,256]{2,1,0:T(8,128)(2,1)S(1)} async-done(((bf16[8,72,256]{2,1,0:T(8,128)(2,1)}), bf16[8,72,256]{2,1,0:T(8,128)(2,1)S(1)}, u32[]{:S(2)}, u32[]{:S(2)}) %all-to-all-start) | async-done | bytes 294944 | tf_op jit(solution)/shard_map/all_to_all | solution.py:364
  150.2 5.2 %all-to-all-start.1 = ((bf16[8,72,256]{2,1,0:T(8,128)(2,1)}), bf16[8,72,256]{2,1,0:T(8,128)(2,1)S(1)}, u32[]{:S(2)}, u32[]{:S(2)}) async-start(bf16[8,72,256]{2,1,0:T(8,128)(2,1)} %bitcast.21), calls=%async_computation.1 | async-start | bytes 589824 | tf_op jit(solution)/shard_map/all_to_all | solution.py:364
  155.4 29.3 %all_gather.22 = bf16[576,256]{1,0:T(8,128)(2,1)} all-gather(bf16[72,256]{1,0:T(8,128)(2,1)S(1)} %multiply_convert_fusion.1), channel_id=1, replica_groups=mesh['tm'=8,'row'=4] {'tm'}, dimensions={0}, use_global_device_ids=true | all-gather | bytes 331776 | tf_op jit(solution)/shard_map/all_gather | solution.py:369
  185.4 26.9 %all_gather.23 = bf16[576,256]{1,0:T(8,128)(2,1)} all-gather(bf16[72,256]{1,0:T(8,128)(2,1)S(1)} %multiply_convert_fusion), channel_id=1, replica_groups=mesh['tm'=8,'row'=4] {'tm'}, dimensions={0}, use_global_device_ids=true | all-gather | bytes 331776 | tf_op jit(solution)/shard_map/all_gather | solution.py:369
  214.0 17.2 %collective-permute-start.4 = (bf16[64,16,256]{2,1,0:T(8,128)(2,1)}, bf16[64,16,256]{2,1,0:T(8,128)(2,1)}, u32[]{:S(2)}, u32[]{:S(2)}) collective-permute-start(bf16[64,16,256]{2,1,0:T(8,128)(2,1)} %get-tuple-element.24), channel_id=1, source_target_pairs={{0,1},{1,2},{2,3},{4,5},{5,6},{6,7},{8,9},{9,10},{10,11},{12,13},{... | collective-permute-start | bytes 1572872 | tf_op jit(solution)/shard_map/ppermute | solution.py:346
  231.1 2.1 collective-permute-start.5
  237.5 4.4 %collective-permute-done.5.down_ref = bf16[64,16,256]{2,1,0:T(8,128)(2,1)} collective-permute-done((bf16[64,16,256]{2,1,0:T(8,128)(2,1)}, bf16[64,16,256]{2,1,0:T(8,128)(2,1)}, u32[]{:S(2)}, u32[]{:S(2)}) %collective-permute-start.5) | collective-permute-done | bytes 524320 | tf_op jit(solution)/shard_map/ppermute | solution.py:347
  242.0 7.5 %outputs_conv.1 = bf16[64,4,16,256]{3,2,1,0:T(8,128)(2,1)} custom-call(bf16[4,64,16,256]{3,2,1,0:T(8,128)(2,1)S(1)} %copy-done.10, bf16[64,16,256]{2,1,0:T(8,128)(2,1)} %collective-permute-done.4.up_ref, bf16[64,16,256]{2,1,0:T(8,128)(2,1)} %collective-permute-done.5.down_ref, bf16[3,768,256]{2,1,0:T(8,128)(2,1)S(1)} %bitcast.48, ...), custom_call_target="tpu_custom_call" | custom-call | flops 4831838208 | bytes 8388608 | tf_op jit(solution)/shard_map/outputs_conv/pallas_call | solution.py:324
  (76 shorter events, 27.5 us)
Async XLA Ops:
  2.4 7.5 %copy-start.2 = (bf16[1,64,4,16,256]{4,3,2,1,0:T(8,128)(2,1)S(1)}, bf16[1,64,4,16,256]{4,3,2,1,0:T(8,128)(2,1)}, u32[]{:S(2)}) copy-start(bf16[1,64,4,16,256]{4,3,2,1,0:T(8,128)(2,1)} %param.11) | copy-start | bytes 6291460
  3.5 29.0 %collective-permute-start = (bf16[64,16,256]{2,1,0:T(8,128)(2,1)}, bf16[64,16,256]{2,1,0:T(8,128)(2,1)}, u32[]{:S(2)}, u32[]{:S(2)}) collective-permute-start(bf16[64,16,256]{2,1,0:T(8,128)(2,1)} %get-tuple-element.28), channel_id=1, source_target_pairs={{0,1},{1,2},{2,3},{4,5},{5,6},{6,7},{8,9},{9,10},{10,11},{12,13},{... | collective-permute-start | bytes 1572872 | tf_op jit(solution)/shard_map/ppermute | solution.py:346
  8.0 24.5 %collective-permute-start.1 = (bf16[64,16,256]{2,1,0:T(8,128)(2,1)}, bf16[64,16,256]{2,1,0:T(8,128)(2,1)}, u32[]{:S(2)}, u32[]{:S(2)}) collective-permute-start(bf16[64,16,256]{2,1,0:T(8,128)(2,1)} %get-tuple-element.27), channel_id=1, source_target_pairs={{1,0},{2,1},{3,2},{5,4},{6,5},{7,6},{9,8},{10,9},{11,10},{13,12},{... | collective-permute-start | bytes 1572872 | tf_op jit(solution)/shard_map/ppermute | solution.py:347
  11.2 53.6 %collective-permute-start.2 = (bf16[64,16,256]{2,1,0:T(8,128)(2,1)}, bf16[64,16,256]{2,1,0:T(8,128)(2,1)}, u32[]{:S(2)}, u32[]{:S(2)}) collective-permute-start(bf16[64,16,256]{2,1,0:T(8,128)(2,1)} %get-tuple-element.26), channel_id=1, source_target_pairs={{0,1},{1,2},{2,3},{4,5},{5,6},{6,7},{8,9},{9,10},{10,11},{12,13},{... | collective-permute-start | bytes 1572872 | tf_op jit(solution)/shard_map/ppermute | solution.py:346
  15.0 49.8 %collective-permute-start.3 = (bf16[64,16,256]{2,1,0:T(8,128)(2,1)}, bf16[64,16,256]{2,1,0:T(8,128)(2,1)}, u32[]{:S(2)}, u32[]{:S(2)}) collective-permute-start(bf16[64,16,256]{2,1,0:T(8,128)(2,1)} %get-tuple-element.25), channel_id=1, source_target_pairs={{1,0},{2,1},{3,2},{5,4},{6,5},{7,6},{9,8},{10,9},{11,10},{13,12},{... | collective-permute-start | bytes 1572872 | tf_op jit(solution)/shard_map/ppermute | solution.py:347
  24.0 8.5 %copy-start.11 = (f32[64,256]{1,0:T(8,128)S(1)}, f32[64,256]{1,0:T(8,128)}, u32[]{:S(2)}) copy-start(f32[64,256]{1,0:T(8,128)} %decay_ref.5) | copy-start | bytes 196612
  32.5 32.4 %copy-start.8 = (bf16[3,768,256]{2,1,0:T(8,128)(2,1)S(1)}, bf16[3,768,256]{2,1,0:T(8,128)(2,1)}, u32[]{:S(2)}) copy-start(bf16[3,768,256]{2,1,0:T(8,128)(2,1)} %copy-done.7) | copy-start | bytes 3538948
  64.8 32.3 %copy-start.4 = (bf16[1,64,4,16,256]{4,3,2,1,0:T(8,128)(2,1)S(1)}, bf16[1,64,4,16,256]{4,3,2,1,0:T(8,128)(2,1)}, u32[]{:S(2)}) copy-start(bf16[1,64,4,16,256]{4,3,2,1,0:T(8,128)(2,1)} %param.6) | copy-start | bytes 6291460
  106.0 18.8 %collective-permute-start.6 = (bf16[1152,256]{1,0:T(8,128)(2,1)S(1)}, bf16[1152,256]{1,0:T(8,128)(2,1)S(1)}, u32[]{:S(2)}, u32[]{:S(2)}) collective-permute-start(bf16[1152,256]{1,0:T(8,128)(2,1)S(1)} %dynamic-slice_convert_fusion.1), channel_id=1, source_target_pairs={{0,1},{1,0},{2,3},{3,2},{4,5},{5,4},{6,7},{7,6},{8,9},{9,8},{10,11... | collective-permute-start | bytes 1769480 | tf_op jit(solution)/shard_map/ppermute | solution.py:360
  124.7 4.4 %collective-permute-start.10 = (bf16[1152,256]{1,0:T(8,128)(2,1)S(1)}, bf16[1152,256]{1,0:T(8,128)(2,1)S(1)}, u32[]{:S(2)}, u32[]{:S(2)}) collective-permute-start(bf16[1152,256]{1,0:T(8,128)(2,1)S(1)} %dynamic-slice_convert_fusion), channel_id=1, source_target_pairs={{0,1},{1,0},{2,3},{3,2},{4,5},{5,4},{6,7},{7,6},{8,9},{9,8},{10,11... | collective-permute-start | bytes 1769480 | tf_op jit(solution)/shard_map/ppermute | solution.py:360
  126.0 10.5 %collective-permute-start.7 = (bf16[576,256]{1,0:T(8,128)(2,1)S(1)}, bf16[576,256]{1,0:T(8,128)(2,1)S(1)}, u32[]{:S(2)}, u32[]{:S(2)}) collective-permute-start(bf16[576,256]{1,0:T(8,128)(2,1)S(1)} %dynamic-slice_convert_fusion.3), channel_id=1, source_target_pairs={{0,2},{1,3},{2,0},{3,1},{4,6},{5,7},{6,4},{7,5},{8,10},{9,11},{10,... | collective-permute-start | bytes 884744 | tf_op jit(solution)/shard_map/ppermute | solution.py:360
  129.3 13.5 %collective-permute-start.11 = (bf16[576,256]{1,0:T(8,128)(2,1)S(1)}, bf16[576,256]{1,0:T(8,128)(2,1)S(1)}, u32[]{:S(2)}, u32[]{:S(2)}) collective-permute-start(bf16[576,256]{1,0:T(8,128)(2,1)S(1)} %dynamic-slice_convert_fusion.2), channel_id=1, source_target_pairs={{0,2},{1,3},{2,0},{3,1},{4,6},{5,7},{6,4},{7,5},{8,10},{9,11},{10,... | collective-permute-start | bytes 884744 | tf_op jit(solution)/shard_map/ppermute | solution.py:360
  137.2 12.9 %all-to-all-start = ((bf16[8,72,256]{2,1,0:T(8,128)(2,1)}), bf16[8,72,256]{2,1,0:T(8,128)(2,1)S(1)}, u32[]{:S(2)}, u32[]{:S(2)}) async-start(bf16[8,72,256]{2,1,0:T(8,128)(2,1)} %bitcast.18), calls=%async_computation | async-start | bytes 589824 | tf_op jit(solution)/shard_map/all_to_all | solution.py:364
  143.6 69.4 %copy-start.10 = (bf16[4,64,16,256]{3,2,1,0:T(8,128)(2,1)S(1)}, bf16[4,64,16,256]{3,2,1,0:T(8,128)(2,1)}, u32[]{:S(2)}) copy-start(bf16[4,64,16,256]{3,2,1,0:T(8,128)(2,1)} %copy-done.9) | copy-start | bytes 6291460
  150.2 35.1 %all-to-all-start.1 = ((bf16[8,72,256]{2,1,0:T(8,128)(2,1)}), bf16[8,72,256]{2,1,0:T(8,128)(2,1)S(1)}, u32[]{:S(2)}, u32[]{:S(2)}) async-start(bf16[8,72,256]{2,1,0:T(8,128)(2,1)} %bitcast.21), calls=%async_computation.1 | async-start | bytes 589824 | tf_op jit(solution)/shard_map/all_to_all | solution.py:364
  184.8 48.5 %collective-permute-start.8 = (bf16[576,256]{1,0:T(8,128)(2,1)}, bf16[576,256]{1,0:T(8,128)(2,1)}, u32[]{:S(2)}, u32[]{:S(2)}) collective-permute-start(bf16[576,256]{1,0:T(8,128)(2,1)} %all_gather.22), channel_id=1, source_target_pairs={{0,2},{1,3},{2,0},{3,1},{4,6},{5,7},{6,4},{7,5},{8,10},{9,11},{10,... | collective-permute-start | bytes 884744 | tf_op jit(solution)/shard_map/ppermute | solution.py:375
  212.3 22.6 %collective-permute-start.12 = (bf16[576,256]{1,0:T(8,128)(2,1)}, bf16[576,256]{1,0:T(8,128)(2,1)}, u32[]{:S(2)}, u32[]{:S(2)}) collective-permute-start(bf16[576,256]{1,0:T(8,128)(2,1)} %all_gather.23), channel_id=1, source_target_pairs={{0,2},{1,3},{2,0},{3,1},{4,6},{5,7},{6,4},{7,5},{8,10},{9,11},{10,... | collective-permute-start | bytes 884744 | tf_op jit(solution)/shard_map/ppermute | solution.py:375
  212.9 29.0 %copy-start.15 = (bf16[3,3,256,256]{3,2,1,0:T(8,128)(2,1)S(1)}, bf16[3,3,256,256]{3,2,1,0:T(8,128)(2,1)}, u32[]{:S(2)}) copy-start(bf16[3,3,256,256]{3,2,1,0:T(8,128)(2,1)} %w_ref.1) | copy-start | bytes 3538948
  214.0 23.6 %collective-permute-start.4 = (bf16[64,16,256]{2,1,0:T(8,128)(2,1)}, bf16[64,16,256]{2,1,0:T(8,128)(2,1)}, u32[]{:S(2)}, u32[]{:S(2)}) collective-permute-start(bf16[64,16,256]{2,1,0:T(8,128)(2,1)} %get-tuple-element.24), channel_id=1, source_target_pairs={{0,1},{1,2},{2,3},{4,5},{5,6},{6,7},{8,9},{9,10},{10,11},{12,13},{... | collective-permute-start | bytes 1572872 | tf_op jit(solution)/shard_map/ppermute | solution.py:346
  231.1 10.8 %collective-permute-start.5 = (bf16[64,16,256]{2,1,0:T(8,128)(2,1)}, bf16[64,16,256]{2,1,0:T(8,128)(2,1)}, u32[]{:S(2)}, u32[]{:S(2)}) collective-permute-start(bf16[64,16,256]{2,1,0:T(8,128)(2,1)} %get-tuple-element.23), channel_id=1, source_target_pairs={{1,0},{2,1},{3,2},{5,4},{6,5},{7,6},{9,8},{10,9},{11,10},{13,12},{... | collective-permute-start | bytes 1572872 | tf_op jit(solution)/shard_map/ppermute | solution.py:347
  233.2 8.7 %copy-start.5 = (bf16[1,64,4,16,256]{4,3,2,1,0:T(8,128)(2,1)S(1)}, bf16[1,64,4,16,256]{4,3,2,1,0:T(8,128)(2,1)}, u32[]{:S(2)}) copy-start(bf16[1,64,4,16,256]{4,3,2,1,0:T(8,128)(2,1)} %param.6) | copy-start | bytes 6291460
  233.3 8.7 %copy-start.16 = (f32[256]{0:T(256)S(1)}, f32[256]{0:T(256)}, u32[]{:S(2)}) copy-start(f32[256]{0:T(256)} %param.10) | copy-start | bytes 3076
  234.8 14.7 %collective-permute-start.9 = (bf16[1152,256]{1,0:T(8,128)(2,1)S(1)}, bf16[1152,256]{1,0:T(8,128)(2,1)S(1)}, u32[]{:S(2)}, u32[]{:S(2)}) collective-permute-start(bf16[1152,256]{1,0:T(8,128)(2,1)S(1)} %maximum_select_fusion.2), channel_id=1, source_target_pairs={{0,1},{1,0},{2,3},{3,2},{4,5},{5,4},{6,7},{7,6},{8,9},{9,8},{10,11... | collective-permute-start | bytes 1769480 | tf_op jit(solution)/shard_map/ppermute | solution.py:375
  236.3 15.2 %collective-permute-start.13 = (bf16[1152,256]{1,0:T(8,128)(2,1)S(1)}, bf16[1152,256]{1,0:T(8,128)(2,1)S(1)}, u32[]{:S(2)}, u32[]{:S(2)}) collective-permute-start(bf16[1152,256]{1,0:T(8,128)(2,1)S(1)} %maximum_select_fusion.3), channel_id=1, source_target_pairs={{0,1},{1,0},{2,3},{3,2},{4,5},{5,4},{6,7},{7,6},{8,9},{9,8},{10,11... | collective-permute-start | bytes 1769480 | tf_op jit(solution)/shard_map/ppermute | solution.py:375
  (9 other events, 31.1 us)
where the time goes:
time: 254 us; the launch traced here: 253 us
  blocking collectives  108 us (43%)
  starting transfers between devices  57.9 us (23%)
  Pallas kernels  43.8 us (17%)
  waiting for transfers between devices  18.4 us (7%)
  local copies, waits for them, and re-layouts  15.3 us (6%)
  other arithmetic  8.67 us (3%)
    all_gather x2, blocking collectives, gathered(): whole = lax.all_gather(share, 'tm', axis=0, tiled=True)  56.3 us
    all_gather x1, blocking collectives, per_device(): all_ends = lax.all_gather(ends, 'tm')  26.2 us
    all_gather x1, blocking collectives, per_device(): all_starts = lax.all_gather(starts, 'tm')  25.7 us
    ppermute x3, starting transfers between devices, row_halo(): up = lax.ppermute(last, 'row', [(i, i + 1) for i in range(count - 1)])  25.4 us
    ppermute x4, starting transfers between devices, reduced_share(): grad = kept + lax.ppermute(sent, 'row', pairs).astype(F32)  14.3 us
    unnamed x36, local copies, waits for them, and re-layouts  12 us
    all_to_all x2, starting transfers between devices, reduced_share(): parts = lax.all_to_all(parts, 'tm', 0, 0)  10.5 us
    pallas_call x1, Pallas kernels, kernel_grads(): pl.pallas_call(in_grad_kernel, grid=(frames // block,), in_specs=lead + [...  8.83 us
  transfers between devices with their start and end apart: 16, of which 5 were waited for; matrix products, arithmetic and copies ran while one was open for 4% of the time, Pallas kernels for 12%

commit v1 on v0

--- a/solution.py
+++ b/solution.py
@@ -12,7 +12,7 @@
 F32 = jnp.float32
 
 
-def params(mib=44):
+def params(mib=20):
     return pltpu.CompilerParams(
         dimension_semantics=("arbitrary",), vmem_limit_bytes=mib * 1024 * 1024
     )
@@ -61,7 +61,7 @@
     interior_body(x_ref, w_ref, out_ref, s_ref)
 
 
-def interior_flipped_kernel(x_ref, w_ref, out_ref, wt_ref, s_ref):
+def interior_flipped_kernel(x_ref, w_ref, after_ref, out_ref, wt_ref, s_ref):
     @pl.when(pl.program_id(0) == 0)
     def _():
         for i in range(3):
@@ -72,7 +72,7 @@
     interior_body(x_ref, wt_ref, out_ref, s_ref)
 
 
-def interior_conv(x, w, flipped, block):
+def interior_conv(x, w, flipped, block, after=None):
     frames, rows, width, c = x.shape
     p = w.shape[2] if flipped else w.shape[3]
     part_shape = jax.ShapeDtypeStruct((rows, frames, width, p), F32)
@@ -85,14 +85,18 @@
         return pl.pallas_call(
             interior_flipped_kernel,
             grid=(frames // block,),
-            in_specs=[x_spec, pl.BlockSpec(w.shape, lambda b: (0, 0, 0, 0))],
+            in_specs=[
+                x_spec,
+                pl.BlockSpec(w.shape, lambda b: (0, 0, 0, 0)),
+                pl.BlockSpec(memory_space=pl.ANY),
+            ],
             out_specs=[part_spec, taps_spec],
             out_shape=[part_shape, jax.ShapeDtypeStruct((3, 3 * c, p), BF16)],
             scratch_shapes=scratch,
             compiler_params=params(),
             cost_estimate=estimate,
             name="interior_cot",
-        )(x, w)
+        )(x, w, after)
     taps = w.reshape(3, 3 * c, p)
     part = pl.pallas_call(
         interior_plain_kernel,
@@ -204,7 +208,7 @@
     s_ref[rows + 1] = shifted(flat(down_ref[...]), width)
 
 
-def out_grad_kernel(place_ref, ends_ref, local_ref, product_ref, cot_ref, up_ref, down_ref, low_ref, grad_ref, s_ref, total_ref):
+def out_grad_kernel(place_ref, ends_ref, local_ref, product_ref, cot_ref, up_ref, down_ref, low_ref, first_ref, last_ref, grad_ref, s_ref, total_ref):
     rows, frames, width, p = local_ref.shape
     c = cot_ref.shape[-1]
 
@@ -220,6 +224,10 @@
         state = local_ref[r] + product[:, None, :] * total_ref[r * width : (r + 1) * width][None]
         low = state.astype(BF16)
         low_ref[r] = low
+        if r == 0:
+            first_ref[...] = low
+        if r == rows - 1:
+            last_ref[...] = low
         turned.append(flat(low).T)
     turned = jnp.concatenate(turned, axis=1)
     for i in range(3):
@@ -228,7 +236,7 @@
             grad_ref[3 * i + j] += gain[:, (2 - j) * c : (3 - j) * c]
 
 
-def in_grad_kernel(place_ref, ends_ref, local_ref, product_ref, decay_ref, x_ref, up_ref, down_ref, grad_ref, s_ref, total_ref, sum_ref):
+def in_grad_kernel(place_ref, ends_ref, local_ref, product_ref, decay_ref, x_ref, up_ref, down_ref, after_ref, grad_ref, s_ref, total_ref, sum_ref):
     rows, frames, width, p = local_ref.shape
     c = x_ref.shape[-1]
 
@@ -256,7 +264,7 @@
                 grad_ref[3 * i + j] = sum_ref[i, :, j * c : (j + 1) * c].T
 
 
-def kernel_grads(place, ends, local, product, x, up, down, decays, block):
+def kernel_grads(place, ends, local, product, x, up, down, decays, block, after=None):
     rows, frames, width, p = local.shape
     c = x.shape[-1]
     halo_spec = pl.BlockSpec((block, width, c), lambda b: (b, 0, 0))
@@ -280,9 +288,16 @@
             out_grad_kernel,
             grid=(frames // block,),
             in_specs=lead + tail,
-            out_specs=[local_spec, pl.BlockSpec((9, p, c), lambda b: (0, 0, 0))],
+            out_specs=[
+                local_spec,
+                pl.BlockSpec((block, width, p), lambda b: (b, 0, 0)),
+                pl.BlockSpec((block, width, p), lambda b: (b, 0, 0)),
+                pl.BlockSpec((9, p, c), lambda b: (0, 0, 0)),
+            ],
             out_shape=[
                 jax.ShapeDtypeStruct(local.shape, BF16),
+                jax.ShapeDtypeStruct((frames, width, p), BF16),
+                jax.ShapeDtypeStruct((frames, width, p), BF16),
                 jax.ShapeDtypeStruct((9, p, c), F32),
             ],
             scratch_shapes=scratch,
@@ -293,14 +308,14 @@
     return pl.pallas_call(
         in_grad_kernel,
         grid=(frames // block,),
-        in_specs=lead + [frame_spec] + tail,
+        in_specs=lead + [frame_spec] + tail + [pl.BlockSpec(memory_space=pl.ANY)],
         out_specs=pl.BlockSpec((9, c, p), lambda b: (0, 0, 0)),
         out_shape=jax.ShapeDtypeStruct((9, c, p), F32),
         scratch_shapes=scratch + [pltpu.VMEM((3, p, 3 * c), F32)],
         compiler_params=params(),
         cost_estimate=estimate,
         name="in_grad",
-    )(place, ends, local, product, decays, x, up, down)
+    )(place, ends, local, product, decays, x, up, down, after)
 
 
 def outputs_kernel(low_ref, up_ref, down_ref, w_ref, x_ref, skip_ref, out_ref, s_ref):
@@ -341,78 +356,125 @@
     )(low, up, down, taps, x, skip)
 
 
+def edge_rows_kernel(x_ref, after_ref, first_ref, last_ref, sems):
+    rows = x_ref.shape[1]
+    first = pltpu.make_async_copy(x_ref.at[:, 0], first_ref, sems.at[0])
+    last = pltpu.make_async_copy(x_ref.at[:, rows - 1], last_ref, sems.at[1])
+    first.start()
+    last.start()
+    first.wait()
+    last.wait()
+
+
+def edge_rows(x, after):
+    frames, rows, width, c = x.shape
+    anywhere = pl.BlockSpec(memory_space=pl.ANY)
+    line = jax.ShapeDtypeStruct((frames, width, c), x.dtype)
+    return pl.pallas_call(
+        edge_rows_kernel,
+        in_specs=[anywhere, anywhere],
+        out_specs=[anywhere, anywhere],
+        out_shape=[line, line],
+        scratch_shapes=[pltpu.SemaphoreType.DMA((2,))],
+        compiler_params=pltpu.CompilerParams(vmem_limit_bytes=2**20),
+        cost_estimate=cost(0, 2**21),
+        name="edge_rows",
+    )(x, after)
+
+
 def row_halo(first, last):
-    count = lax.axis_size("row")
-    up = lax.ppermute(last, "row", [(i, i + 1) for i in range(count - 1)])
-    down = lax.ppermute(first, "row", [(i + 1, i) for i in range(count - 1)])
+    axes = ("y", "core")
+    count = lax.axis_size("y") * lax.axis_size("core")
+    up = lax.ppermute(last, axes, [(i, i + 1) for i in range(count - 1)])
+    down = lax.ppermute(first, axes, [(i + 1, i) for i in range(count - 1)])
     return up, down
 
 
+def spread(block, axes):
+    count = math.prod(lax.axis_size(name) for name in axes)
+    return lax.all_to_all(jnp.broadcast_to(block[None], (count,) + block.shape), axes, 0, 0)
+
+
+def scattered_sum(part, axes):
+    count = math.prod(lax.axis_size(name) for name in axes)
+    parts = part.astype(BF16).reshape(count, part.shape[0] // count, part.shape[1])
+    return jnp.sum(lax.all_to_all(parts, axes, 0, 0).astype(F32), axis=0)
+
+
+CORES = [(0, 1), (1, 0)]
+
+
 def reduced_share(grad, scale):
-    place = lax.axis_index("row")
-    bit = 1
-    while bit < lax.axis_size("row"):
-        half = grad.shape[0] // 2
-        side = (place // bit) % 2
-        sent = lax.dynamic_slice_in_dim(grad, (1 - side) * half, half, 0).astype(BF16)
-        kept = lax.dynamic_slice_in_dim(grad, side * half, half, 0)
-        pairs = [(i, i ^ bit) for i in range(lax.axis_size("row"))]
-        grad = kept + lax.ppermute(sent, "row", pairs).astype(F32)
-        bit *= 2
-    count = lax.axis_size("tm")
-    parts = grad.astype(BF16).reshape(count, grad.shape[0] // count, grad.shape[1])
-    parts = lax.all_to_all(parts, "tm", 0, 0)
-    return (jnp.sum(parts.astype(F32), axis=0) * scale).astype(BF16)
+    side = lax.axis_index("core")
+    half = grad.shape[0] // 2
+    sent = lax.dynamic_slice_in_dim(grad, (1 - side) * half, half, 0).astype(BF16)
+    kept = lax.dynamic_slice_in_dim(grad, side * half, half, 0)
+    part = kept + lax.ppermute(sent, "core", CORES).astype(F32)
+    part = scattered_sum(part, ("x", "y"))
+    part = scattered_sum(part, ("a",))
+    return (part * scale).astype(BF16)
+
+
+def merge_kernel(side_ref, own_ref, other_ref, out_ref):
+    @pl.when(pl.program_id(0) == 0)
+    def _():
+        out_ref[...] = own_ref[...].astype(F32)
+
+    @pl.when(pl.program_id(0) == 1)
+    def _():
+        out_ref[...] = other_ref[...].astype(F32)
 
 
 def gathered(share):
-    whole = lax.all_gather(share, "tm", axis=0, tiled=True)
-    place = lax.axis_index("row")
-    bit = lax.axis_size("row") // 2
-    while bit >= 1:
-        side = (place // bit) % 2
-        pairs = [(i, i ^ bit) for i in range(lax.axis_size("row"))]
-        other = lax.ppermute(whole, "row", pairs)
-        whole = jnp.where(
-            side == 0,
-            jnp.concatenate([whole, other], axis=0),
-            jnp.concatenate([other, whole], axis=0),
-        )
-        bit //= 2
-    return whole.astype(F32)
+    part = flat(spread(share, ("a",)))
+    own = flat(spread(part, ("x", "y")))
+    other = lax.ppermute(own, "core", CORES)
+    side = lax.axis_index("core").astype(jnp.int32).reshape(1)
+    half, c = own.shape
+    part_spec = pl.BlockSpec((half, c), lambda g, side: (0, 0))
+    return pl.pallas_call(
+        merge_kernel,
+        grid_spec=pltpu.PrefetchScalarGridSpec(
+            num_scalar_prefetch=1,
+            grid=(2,),
+            in_specs=[part_spec, part_spec],
+            out_specs=pl.BlockSpec((half, c), lambda g, side: (jnp.bitwise_xor(g, side[0]), 0)),
+        ),
+        out_shape=jax.ShapeDtypeStruct((2 * half, c), F32),
+        compiler_params=params(8),
+        cost_estimate=cost(0, 10 * half * c),
+        name="merge",
+    )(side, own, other)
 
 
 def per_device(inputs, decays, in_kernel, out_kernel, skip, cotangent):
     clips, frames, rows, width, c = inputs.shape
     p = in_kernel.shape[3]
     block = 16
-    grad_scale = 1.0 / math.sqrt(
-        clips * frames * lax.axis_size("tm") * rows * lax.axis_size("row") * width
-    )
+    devices = math.prod(lax.axis_size(name) for name in ("a", "x", "y", "core"))
+    grad_scale = 1.0 / math.sqrt(clips * frames * rows * width * devices)
     x = inputs.reshape(frames, rows, width, c)
     cot = cotangent.reshape(frames, rows, width, c)
-    place = lax.axis_index("tm").astype(jnp.int32).reshape(1)
-
-    cot_up, cot_down = row_halo(cot[:, 0], cot[:, rows - 1])
-    x_up, x_down = row_halo(x[:, 0], x[:, rows - 1])
-
-    cot_part, cot_taps = interior_conv(cot, out_kernel, True, block)
+    place = lax.axis_index(("a", "x")).astype(jnp.int32).reshape(1)
+
+    x_up, x_down = row_halo(*edge_rows(x, decays))
     x_part, x_taps = interior_conv(x, in_kernel, False, block)
-
+    cot_up, cot_down = row_halo(*edge_rows(cot, x_part))
     states, running, ends = local_scan(x_part, x_up, x_down, x_taps, decays, False, block)
-    all_ends = lax.all_gather(ends, "tm")
+    all_ends = spread(ends, ("a", "x"))
+    cot_part, cot_taps = interior_conv(cot, out_kernel, True, block, ends)
     adjoint, trailing, starts = local_scan(
         cot_part, cot_up, cot_down, cot_taps, decays, True, block
     )
-    all_starts = lax.all_gather(starts, "tm")
-
-    low, out_grad = kernel_grads(
+    all_starts = spread(starts, ("a", "x"))
+
+    low, low_first, low_last, out_grad = kernel_grads(
         place, all_ends, states, running, cot, cot_up, cot_down, None, block
     )
-    low_up, low_down = row_halo(low[0], low[rows - 1])
     out_share = reduced_share(out_grad.reshape(-1, c), grad_scale)
+    low_up, low_down = row_halo(low_first, low_last)
     in_grad = kernel_grads(
-        place, all_starts, adjoint, trailing, x, x_up, x_down, decays, block
+        place, all_starts, adjoint, trailing, x, x_up, x_down, decays, block, low_first
     )
     in_share = reduced_share(in_grad.reshape(-1, p), grad_scale)
 
@@ -427,17 +489,16 @@
 
 
 def solution(mesh):
+    frames = mesh.shape["tm"]
+    rows = mesh.shape["row"]
+    fine = jax.sharding.Mesh(
+        mesh.devices.reshape(frames // 2, 2, rows // 2, 2), ("a", "x", "y", "core")
+    )
+    cells = P(None, ("a", "x"), ("y", "core"), None, None)
     return jax.shard_map(
         per_device,
-        mesh=mesh,
-        in_specs=(
-            P(None, "tm", "row", None, None),
-            P("tm", None),
-            P(),
-            P(),
-            P(),
-            P(None, "tm", "row", None, None),
-        ),
-        out_specs=(P(None, "tm", "row", None, None), P(), P()),
+        mesh=fine,
+        in_specs=(cells, P(("a", "x"), None), P(), P(), P(), cells),
+        out_specs=(cells, P(), P()),
         check_vma=False,
     )

time: 254 us -> 204 us (0.80)
  blocking collectives: 108 us -> 18.4 us
  waiting for transfers between devices: 18.4 us -> 41.8 us
  local copies, waits for them, and re-layouts: 15.3 us -> 35.3 us
  other arithmetic: 8.67 us -> 4.77 us
    all_gather x4 -> x0, blocking collectives: 108 us -> none  [the longest x2 56.3 us: gathered(): whole = lax.all_gather(share, 'tm', axis=0, tiled=True)]
    all_to_all x2 -> x8, starting transfers between devices: 10.5 us -> 32.9 us  [the longest x4 18.1 us: spread(): lax.all_to_all(jnp.broadcast_to(block[None], (count,) + block.shape), axe...]
    ppermute x14 -> x10, starting transfers between devices: 47.5 us -> 25.2 us  [the longest x3 17.1 us: row_halo(): up = lax.ppermute(last, axes, [(i, i + 1) for i in range(count - 1)])]
    all_to_all x2 -> x8, waiting for transfers between devices: 6.62 us -> 28.7 us  [the longest x4 23.9 us: scattered_sum(): return jnp.sum(lax.all_to_all(parts, axes, 0, 0).astype(F32), axis=0)]
    all_to_all x0 -> x2, blocking collectives: none -> 18.4 us  [spread(): lax.all_to_all(jnp.broadcast_to(block[None], (count,) + block.shape), axe...]
    unnamed x36 -> x64, local copies, waits for them, and re-layouts: 12 us -> 30.2 us
    pallas_call x0 -> x4, Pallas kernels: none -> 4.4 us  [the longest x2 4.04 us: gathered(): pl.pallas_call(merge_kernel, grid_spec=pltpu.PrefetchScalarGridSpec(num_s...]
    pallas_call x2, Pallas kernels: 8.67 us -> 4.7 us  [local_scan(): pl.pallas_call(functools.partial(scan_kernel, backward), grid=(blocks,),...]
  transfers between devices with their start and end apart: 16 -> 18, of which waited for: 5 -> 10; matrix products, arithmetic and copies ran while one was open for 4% -> 3% of each run, Pallas kernels for 12% -> 15%
where the time goes in v1:
time: 204 us; the launch traced here: 202 us
  starting transfers between devices  58.1 us (28%)
  Pallas kernels  43.1 us (21%)
  waiting for transfers between devices  41.8 us (20%)
  local copies, waits for them, and re-layouts  35.3 us (17%)
  blocking collectives  18.4 us (9%)
  other arithmetic  4.77 us (2%)
    unnamed x64, local copies, waits for them, and re-layouts  30.2 us
    all_to_all x4, waiting for transfers between devices, scattered_sum(): return jnp.sum(lax.all_to_all(parts, axes, 0, 0).astype(F32), axis=0)  23.9 us
    all_to_all x2, blocking collectives, spread(): lax.all_to_all(jnp.broadcast_to(block[None], (count,) + block.shape), axe...  18.4 us
    all_to_all x4, starting transfers between devices, spread(): lax.all_to_all(jnp.broadcast_to(block[None], (count,) + block.shape), axe...  18.1 us
    ppermute x3, starting transfers between devices, row_halo(): up = lax.ppermute(last, axes, [(i, i + 1) for i in range(count - 1)])  17.1 us
    all_to_all x4, starting transfers between devices, scattered_sum(): return jnp.sum(lax.all_to_all(parts, axes, 0, 0).astype(F32), axis=0)  14.8 us
    ppermute x3, waiting for transfers between devices, row_halo(): down = lax.ppermute(first, axes, [(i + 1, i) for i in range(count - 1)])  9.3 us
    pallas_call x1, Pallas kernels, kernel_grads(): pl.pallas_call(in_grad_kernel, grid=(frames // block,), in_specs=lead + [...  8.88 us
  transfers between devices with their start and end apart: 18, of which 10 were waited for; matrix products, arithmetic and copies ran while one was open for 3% of the time, Pallas kernels for 15%

profile of v1, /device:TPU:1, one launch (start us, length us, event | category | flops | bytes accessed | tf_op | source)
XLA Modules:
  0.0 202.5 jit_solution(12705545334299056489)
XLA Ops:
  3.3 4.7 %collective-permute-start = (bf16[64,16,256]{2,1,0:T(8,128)(2,1)S(1)}, bf16[64,16,256]{2,1,0:T(8,128)(2,1)S(1)}, u32[]{:S(2)}, u32[]{:S(2)}) collective-permute-start(bf16[64,16,256]{2,1,0:T(8,128)(2,1)S(1)} %get-tuple-element.19), channel_id=1, source_target_pairs={{0,1},{1,2},{2,3},{4,5},{5,6},{6,7},{8,9},{9,10},{10,11},{12,13},{... | collective-permute-start | bytes 1572872 | tf_op jit(solution)/shard_map/ppermute | solution.py:388
  11.2 5.0 %interior_in.1.part_ref.after_ref = f32[4,64,16,256]{3,2,1,0:T(8,128)S(1)} custom-call(bf16[64,4,16,256]{3,2,1,0:T(8,128)(2,1)S(1)} %bitcast.28, bf16[3,768,256]{2,1,0:T(8,128)(2,1)S(1)} %bitcast.35), custom_call_target="tpu_custom_call" | custom-call | flops 4831838208 | bytes 8388608 | tf_op jit(solution)/shard_map/interior_in/pallas_call | solution.py:101
  23.6 5.5 %all-to-all-start = ((f32[8,72,256]{2,1,0:T(8,128)}), f32[8,72,256]{2,1,0:T(8,128)S(1)}, u32[]{:S(2)}, u32[]{:S(2)}) async-start(f32[8,72,256]{2,1,0:T(8,128)} %broadcast_in_dim.16), calls=%async_computation | async-start | bytes 1179648 | tf_op jit(solution)/shard_map/all_to_all | solution.py:395
  36.0 5.4 %interior_cot.1 = (f32[4,64,16,256]{3,2,1,0:T(8,128)S(1)}, bf16[3,768,256]{2,1,0:T(8,128)(2,1)S(1)}) custom-call(bf16[64,4,16,256]{3,2,1,0:T(8,128)(2,1)S(1)} %bitcast.25, bf16[3,3,256,256]{3,2,1,0:T(8,128)(2,1)S(1)} %copy-done.24, f32[72,256]{1,0:T(8,128)S(1)} %get-tuple-element.21.after_ref), custom_call_target="tpu_custom_call" | custom-call | flops 4831838208 | bytes 8388608 | tf_op jit(solution)/shard_map/interior_cot/pallas_call | solution.py:85
  51.1 5.7 %all-to-all-start.1 = ((f32[8,72,256]{2,1,0:T(8,128)}), f32[8,72,256]{2,1,0:T(8,128)}, u32[]{:S(2)}, u32[]{:S(2)}) async-start(f32[8,72,256]{2,1,0:T(8,128)} %broadcast_in_dim.17), calls=%async_computation.1 | async-start | bytes 1179648 | tf_op jit(solution)/shard_map/all_to_all | solution.py:395
  61.1 7.2 %out_grad.1 = (bf16[4,64,16,256]{3,2,1,0:T(8,128)(2,1)S(1)}, bf16[64,16,256]{2,1,0:T(8,128)(2,1)S(1)}, bf16[64,16,256]{2,1,0:T(8,128)(2,1)S(1)}, f32[9,256,256]{2,1,0:T(8,128)S(1)}) custom-call(s32[1]{0:T(128)} %bitcast.place_ref, f32[8,72,256]{2,1,0:T(8,128)S(1)} %all-to-all-done.ends_ref, f32[4,64,16,256]{3,2,1,0:T(8,128)S(1)} %copy-done.21, ...), custom_call_target="tpu_custom_call" | custom-call | flops 4831838208 | bytes 10485760 | tf_op jit(solution)/shard_map/out_grad/pallas_call | solution.py:287
  78.5 8.9 %in_grad.1 = f32[9,256,256]{2,1,0:T(8,128)S(1)} custom-call(s32[1]{0:T(128)} %bitcast.place_ref, f32[8,72,256]{2,1,0:T(8,128)} %all-to-all-done.1.ends_ref, f32[4,64,16,256]{3,2,1,0:T(8,128)S(1)} %copy-done.23, f32[64,256]{1,0:T(8,128)S(1)} %get-tuple-element.33.product_ref, f32[64,256]{1,0:T(8,128)S(1)} %copy-done.13, ...), custom_call_target="tpu_custom_call" | custom-call | flops 4831838208 | bytes 10485760 | tf_op jit(solution)/shard_map/in_grad/pallas_call | solution.py:308
  94.1 3.5 %all-to-all-start.2 = ((bf16[4,288,256]{2,1,0:T(8,128)(2,1)}), bf16[4,288,256]{2,1,0:T(8,128)(2,1)S(1)}, u32[]{:S(2)}, u32[]{:S(2)}) async-start(bf16[4,288,256]{2,1,0:T(8,128)(2,1)} %bitcast.9), calls=%async_computation.2 | async-start | bytes 1179648 | tf_op jit(solution)/shard_map/all_to_all | solution.py:401
  98.5 7.7 %all-to-all-done.2 = bf16[4,288,256]{2,1,0:T(8,128)(2,1)S(1)} async-done(((bf16[4,288,256]{2,1,0:T(8,128)(2,1)}), bf16[4,288,256]{2,1,0:T(8,128)(2,1)S(1)}, u32[]{:S(2)}, u32[]{:S(2)}) %all-to-all-start.2) | async-done | bytes 589856 | tf_op jit(solution)/shard_map/all_to_all | solution.py:401
  106.3 3.5 %all-to-all-start.6 = ((bf16[4,288,256]{2,1,0:T(8,128)(2,1)}), bf16[4,288,256]{2,1,0:T(8,128)(2,1)S(1)}, u32[]{:S(2)}, u32[]{:S(2)}) async-start(bf16[4,288,256]{2,1,0:T(8,128)(2,1)} %bitcast.15), calls=%async_computation.6 | async-start | bytes 1179648 | tf_op jit(solution)/shard_map/all_to_all | solution.py:401
  110.5 7.4 %all-to-all-done.6 = bf16[4,288,256]{2,1,0:T(8,128)(2,1)S(1)} async-done(((bf16[4,288,256]{2,1,0:T(8,128)(2,1)}), bf16[4,288,256]{2,1,0:T(8,128)(2,1)S(1)}, u32[]{:S(2)}, u32[]{:S(2)}) %all-to-all-start.6) | async-done | bytes 589856 | tf_op jit(solution)/shard_map/all_to_all | solution.py:401
  117.9 4.5 %all-to-all-start.3 = ((bf16[4,72,256]{2,1,0:T(8,128)(2,1)}), bf16[4,72,256]{2,1,0:T(8,128)(2,1)S(1)}, u32[]{:S(2)}, u32[]{:S(2)}) async-start(bf16[4,72,256]{2,1,0:T(8,128)(2,1)} %bitcast.10), calls=%async_computation.3 | async-start | bytes 294912 | tf_op jit(solution)/shard_map/all_to_all | solution.py:401
  123.2 4.0 %all-to-all-done.3 = bf16[4,72,256]{2,1,0:T(8,128)(2,1)S(1)} async-done(((bf16[4,72,256]{2,1,0:T(8,128)(2,1)}), bf16[4,72,256]{2,1,0:T(8,128)(2,1)S(1)}, u32[]{:S(2)}, u32[]{:S(2)}) %all-to-all-start.3) | async-done | bytes 147488 | tf_op jit(solution)/shard_map/all_to_all | solution.py:401
  127.3 3.3 %all-to-all-start.7 = ((bf16[4,72,256]{2,1,0:T(8,128)(2,1)}), bf16[4,72,256]{2,1,0:T(8,128)(2,1)S(1)}, u32[]{:S(2)}, u32[]{:S(2)}) async-start(bf16[4,72,256]{2,1,0:T(8,128)(2,1)} %bitcast.16), calls=%async_computation.7 | async-start | bytes 294912 | tf_op jit(solution)/shard_map/all_to_all | solution.py:401
  130.7 4.7 %all-to-all-done.7 = bf16[4,72,256]{2,1,0:T(8,128)(2,1)S(1)} async-done(((bf16[4,72,256]{2,1,0:T(8,128)(2,1)}), bf16[4,72,256]{2,1,0:T(8,128)(2,1)S(1)}, u32[]{:S(2)}, u32[]{:S(2)}) %all-to-all-start.7) | async-done | bytes 147488 | tf_op jit(solution)/shard_map/all_to_all | solution.py:401
  136.1 3.3 %all-to-all-start.4 = ((bf16[4,72,256]{2,1,0:T(8,128)(2,1)}), bf16[4,72,256]{2,1,0:T(8,128)(2,1)S(1)}, u32[]{:S(2)}, u32[]{:S(2)}) async-start(bf16[4,72,256]{2,1,0:T(8,128)(2,1)} %broadcast_in_dim.18), calls=%async_computation.4 | async-start | bytes 294912 | tf_op jit(solution)/shard_map/all_to_all | solution.py:395
  139.5 4.7 %all-to-all-done.4 = bf16[4,72,256]{2,1,0:T(8,128)(2,1)S(1)} async-done(((bf16[4,72,256]{2,1,0:T(8,128)(2,1)}), bf16[4,72,256]{2,1,0:T(8,128)(2,1)S(1)}, u32[]{:S(2)}, u32[]{:S(2)}) %all-to-all-start.4) | async-done | bytes 147488 | tf_op jit(solution)/shard_map/all_to_all | solution.py:395
  144.2 8.2 %all_to_all.50 = bf16[4,72,256]{2,1,0:T(8,128)(2,1)S(1)} all-to-all(bf16[4,72,256]{2,1,0:T(8,128)(2,1)S(1)} %broadcast_in_dim.21), channel_id=1, replica_groups=mesh['a'=4,'x'=2,'y'=2,'core'=2] {'a'}, dimensions={0} | all-to-all | bytes 294912 | tf_op jit(solution)/shard_map/all_to_all | solution.py:395
  152.5 10.2 %all_to_all.51 = bf16[4,288,256]{2,1,0:T(8,128)(2,1)S(1)} all-to-all(bf16[4,288,256]{2,1,0:T(8,128)(2,1)S(1)} %broadcast_in_dim.20), channel_id=1, replica_groups=mesh['a'=4,'x'=2,'y'=2,'core'=2] {'x','y'}, dimensions={0} | all-to-all | bytes 1179648 | tf_op jit(solution)/shard_map/all_to_all | solution.py:395
  163.5 3.5 %all-to-all-start.9 = ((bf16[4,288,256]{2,1,0:T(8,128)(2,1)}), bf16[4,288,256]{2,1,0:T(8,128)(2,1)S(1)}, u32[]{:S(2)}, u32[]{:S(2)}) async-start(bf16[4,288,256]{2,1,0:T(8,128)(2,1)} %broadcast_in_dim.45), calls=%async_computation.9 | async-start | bytes 1179648 | tf_op jit(solution)/shard_map/all_to_all | solution.py:395
  167.0 10.2 %collective-permute-start.4 = (bf16[64,16,256]{2,1,0:T(8,128)(2,1)}, bf16[64,16,256]{2,1,0:T(8,128)(2,1)}, u32[]{:S(2)}, u32[]{:S(2)}) collective-permute-start(bf16[64,16,256]{2,1,0:T(8,128)(2,1)} %copy-done.28), channel_id=1, source_target_pairs={{0,1},{1,2},{2,3},{4,5},{5,6},{6,7},{8,9},{9,10},{10,11},{12,13},{... | collective-permute-start | bytes 1572872 | tf_op jit(solution)/shard_map/ppermute | solution.py:388
  180.7 3.0 %collective-permute-done.4.up_ref = bf16[64,16,256]{2,1,0:T(8,128)(2,1)} collective-permute-done((bf16[64,16,256]{2,1,0:T(8,128)(2,1)}, bf16[64,16,256]{2,1,0:T(8,128)(2,1)}, u32[]{:S(2)}, u32[]{:S(2)}) %collective-permute-start.4) | collective-permute-done | bytes 524320 | tf_op jit(solution)/shard_map/ppermute | solution.py:388
  183.6 4.4 %collective-permute-done.5.down_ref = bf16[64,16,256]{2,1,0:T(8,128)(2,1)} collective-permute-done((bf16[64,16,256]{2,1,0:T(8,128)(2,1)}, bf16[64,16,256]{2,1,0:T(8,128)(2,1)}, u32[]{:S(2)}, u32[]{:S(2)}) %collective-permute-start.5) | collective-permute-done | bytes 524320 | tf_op jit(solution)/shard_map/ppermute | solution.py:389
  190.9 7.5 %outputs_conv.1 = bf16[64,4,16,256]{3,2,1,0:T(8,128)(2,1)} custom-call(bf16[4,64,16,256]{3,2,1,0:T(8,128)(2,1)S(1)} %copy-done.31, bf16[64,16,256]{2,1,0:T(8,128)(2,1)} %collective-permute-done.4.up_ref, bf16[64,16,256]{2,1,0:T(8,128)(2,1)} %collective-permute-done.5.down_ref, bf16[3,768,256]{2,1,0:T(8,128)(2,1)S(1)} %bitcast.37, ...), custom_call_target="tpu_custom_call" | custom-call | flops 4831838208 | bytes 8388608 | tf_op jit(solution)/shard_map/outputs_conv/pallas_call | solution.py:339
  (105 shorter events, 65.2 us)
Async XLA Ops:
  3.3 13.0 %collective-permute-start = (bf16[64,16,256]{2,1,0:T(8,128)(2,1)S(1)}, bf16[64,16,256]{2,1,0:T(8,128)(2,1)S(1)}, u32[]{:S(2)}, u32[]{:S(2)}) collective-permute-start(bf16[64,16,256]{2,1,0:T(8,128)(2,1)S(1)} %get-tuple-element.19), channel_id=1, source_target_pairs={{0,1},{1,2},{2,3},{4,5},{5,6},{6,7},{8,9},{9,10},{10,11},{12,13},{... | collective-permute-start | bytes 1572872 | tf_op jit(solution)/shard_map/ppermute | solution.py:388
  7.9 10.5 %collective-permute-start.1 = (bf16[64,16,256]{2,1,0:T(8,128)(2,1)S(1)}, bf16[64,16,256]{2,1,0:T(8,128)(2,1)S(1)}, u32[]{:S(2)}, u32[]{:S(2)}) collective-permute-start(bf16[64,16,256]{2,1,0:T(8,128)(2,1)S(1)} %get-tuple-element.20), channel_id=1, source_target_pairs={{1,0},{2,1},{3,2},{5,4},{6,5},{7,6},{9,8},{10,9},{11,10},{13,12},{... | collective-permute-start | bytes 1572872 | tf_op jit(solution)/shard_map/ppermute | solution.py:389
  11.1 7.3 %copy-start.11 = (bf16[3,3,256,256]{3,2,1,0:T(8,128)(2,1)S(1)}, bf16[3,3,256,256]{3,2,1,0:T(8,128)(2,1)}, u32[]{:S(2)}) copy-start(bf16[3,3,256,256]{3,2,1,0:T(8,128)(2,1)} %param.8) | copy-start | bytes 3538948
  11.1 7.3 %copy-start.13 = (f32[64,256]{1,0:T(8,128)S(1)}, f32[64,256]{1,0:T(8,128)}, u32[]{:S(2)}) copy-start(f32[64,256]{1,0:T(8,128)} %decay_ref.5) | copy-start | bytes 196612
  18.4 10.7 %copy-start.2 = (bf16[1,64,4,16,256]{4,3,2,1,0:T(8,128)(2,1)S(1)}, bf16[1,64,4,16,256]{4,3,2,1,0:T(8,128)(2,1)}, u32[]{:S(2)}) copy-start(bf16[1,64,4,16,256]{4,3,2,1,0:T(8,128)(2,1)} %param.11) | copy-start | bytes 6291460
  23.6 26.6 %all-to-all-start = ((f32[8,72,256]{2,1,0:T(8,128)}), f32[8,72,256]{2,1,0:T(8,128)S(1)}, u32[]{:S(2)}, u32[]{:S(2)}) async-start(f32[8,72,256]{2,1,0:T(8,128)} %broadcast_in_dim.16), calls=%async_computation | async-start | bytes 1179648 | tf_op jit(solution)/shard_map/all_to_all | solution.py:395
  31.5 10.0 %collective-permute-start.2 = (bf16[64,16,256]{2,1,0:T(8,128)(2,1)S(1)}, bf16[64,16,256]{2,1,0:T(8,128)(2,1)S(1)}, u32[]{:S(2)}, u32[]{:S(2)}) collective-permute-start(bf16[64,16,256]{2,1,0:T(8,128)(2,1)S(1)} %get-tuple-element.24), channel_id=1, source_target_pairs={{0,1},{1,2},{2,3},{4,5},{5,6},{6,7},{8,9},{9,10},{10,11},{12,13},{... | collective-permute-start | bytes 1572872 | tf_op jit(solution)/shard_map/ppermute | solution.py:388
  33.7 10.5 %collective-permute-start.3 = (bf16[64,16,256]{2,1,0:T(8,128)(2,1)S(1)}, bf16[64,16,256]{2,1,0:T(8,128)(2,1)S(1)}, u32[]{:S(2)}, u32[]{:S(2)}) collective-permute-start(bf16[64,16,256]{2,1,0:T(8,128)(2,1)S(1)} %get-tuple-element.25), channel_id=1, source_target_pairs={{1,0},{2,1},{3,2},{5,4},{6,5},{7,6},{9,8},{10,9},{11,10},{13,12},{... | collective-permute-start | bytes 1572872 | tf_op jit(solution)/shard_map/ppermute | solution.py:389
  51.1 21.5 %all-to-all-start.1 = ((f32[8,72,256]{2,1,0:T(8,128)}), f32[8,72,256]{2,1,0:T(8,128)}, u32[]{:S(2)}, u32[]{:S(2)}) async-start(f32[8,72,256]{2,1,0:T(8,128)} %broadcast_in_dim.17), calls=%async_computation.1 | async-start | bytes 1179648 | tf_op jit(solution)/shard_map/all_to_all | solution.py:395
  78.4 11.2 %copy-start.8 = (f32[9,256,256]{2,1,0:T(8,128)S(1)}, f32[9,256,256]{2,1,0:T(8,128)}, u32[]{:S(2)}) copy-start(f32[9,256,256]{2,1,0:T(8,128)} %copy-done.7) | copy-start | bytes 7077892
  89.6 2.2 %collective-permute-start.6 = (bf16[1152,256]{1,0:T(8,128)(2,1)}, bf16[1152,256]{1,0:T(8,128)(2,1)S(1)}, u32[]{:S(2)}, u32[]{:S(2)}) collective-permute-start(bf16[1152,256]{1,0:T(8,128)(2,1)} %dynamic-slice_convert_fusion.1), channel_id=1, source_target_pairs={{0,1},{1,0},{2,3},{3,2},{4,5},{5,4},{6,7},{7,6},{8,9},{9,8},{10,11... | collective-permute-start | bytes 1769480 | tf_op jit(solution)/shard_map/ppermute | solution.py:412
  90.5 7.0 %collective-permute-start.8 = (bf16[1152,256]{1,0:T(8,128)(2,1)}, bf16[1152,256]{1,0:T(8,128)(2,1)S(1)}, u32[]{:S(2)}, u32[]{:S(2)}) collective-permute-start(bf16[1152,256]{1,0:T(8,128)(2,1)} %dynamic-slice_convert_fusion), channel_id=1, source_target_pairs={{0,1},{1,0},{2,3},{3,2},{4,5},{5,4},{6,7},{7,6},{8,9},{9,8},{10,11... | collective-permute-start | bytes 1769480 | tf_op jit(solution)/shard_map/ppermute | solution.py:412
  94.1 12.2 %all-to-all-start.2 = ((bf16[4,288,256]{2,1,0:T(8,128)(2,1)}), bf16[4,288,256]{2,1,0:T(8,128)(2,1)S(1)}, u32[]{:S(2)}, u32[]{:S(2)}) async-start(bf16[4,288,256]{2,1,0:T(8,128)(2,1)} %bitcast.9), calls=%async_computation.2 | async-start | bytes 1179648 | tf_op jit(solution)/shard_map/all_to_all | solution.py:401
  106.3 11.7 %all-to-all-start.6 = ((bf16[4,288,256]{2,1,0:T(8,128)(2,1)}), bf16[4,288,256]{2,1,0:T(8,128)(2,1)S(1)}, u32[]{:S(2)}, u32[]{:S(2)}) async-start(bf16[4,288,256]{2,1,0:T(8,128)(2,1)} %bitcast.15), calls=%async_computation.6 | async-start | bytes 1179648 | tf_op jit(solution)/shard_map/all_to_all | solution.py:401
  117.9 9.4 %all-to-all-start.3 = ((bf16[4,72,256]{2,1,0:T(8,128)(2,1)}), bf16[4,72,256]{2,1,0:T(8,128)(2,1)S(1)}, u32[]{:S(2)}, u32[]{:S(2)}) async-start(bf16[4,72,256]{2,1,0:T(8,128)(2,1)} %bitcast.10), calls=%async_computation.3 | async-start | bytes 294912 | tf_op jit(solution)/shard_map/all_to_all | solution.py:401
  127.3 8.1 %all-to-all-start.7 = ((bf16[4,72,256]{2,1,0:T(8,128)(2,1)}), bf16[4,72,256]{2,1,0:T(8,128)(2,1)S(1)}, u32[]{:S(2)}, u32[]{:S(2)}) async-start(bf16[4,72,256]{2,1,0:T(8,128)(2,1)} %bitcast.16), calls=%async_computation.7 | async-start | bytes 294912 | tf_op jit(solution)/shard_map/all_to_all | solution.py:401
  136.1 8.1 %all-to-all-start.4 = ((bf16[4,72,256]{2,1,0:T(8,128)(2,1)}), bf16[4,72,256]{2,1,0:T(8,128)(2,1)S(1)}, u32[]{:S(2)}, u32[]{:S(2)}) async-start(bf16[4,72,256]{2,1,0:T(8,128)(2,1)} %broadcast_in_dim.18), calls=%async_computation.4 | async-start | bytes 294912 | tf_op jit(solution)/shard_map/all_to_all | solution.py:395
  144.2 43.8 %copy-start.6 = (bf16[1,64,4,16,256]{4,3,2,1,0:T(8,128)(2,1)S(1)}, bf16[1,64,4,16,256]{4,3,2,1,0:T(8,128)(2,1)}, u32[]{:S(2)}) copy-start(bf16[1,64,4,16,256]{4,3,2,1,0:T(8,128)(2,1)} %param.6) | copy-start | bytes 6291460
  144.2 43.8 %copy-start.29 = (f32[256]{0:T(256)S(1)}, f32[256]{0:T(256)}, u32[]{:S(2)}) copy-start(f32[256]{0:T(256)} %param.10) | copy-start | bytes 3076
  163.5 15.7 %all-to-all-start.9 = ((bf16[4,288,256]{2,1,0:T(8,128)(2,1)}), bf16[4,288,256]{2,1,0:T(8,128)(2,1)S(1)}, u32[]{:S(2)}, u32[]{:S(2)}) async-start(bf16[4,288,256]{2,1,0:T(8,128)(2,1)} %broadcast_in_dim.45), calls=%async_computation.9 | async-start | bytes 1179648 | tf_op jit(solution)/shard_map/all_to_all | solution.py:395
  167.0 16.7 %collective-permute-start.4 = (bf16[64,16,256]{2,1,0:T(8,128)(2,1)}, bf16[64,16,256]{2,1,0:T(8,128)(2,1)}, u32[]{:S(2)}, u32[]{:S(2)}) collective-permute-start(bf16[64,16,256]{2,1,0:T(8,128)(2,1)} %copy-done.28), channel_id=1, source_target_pairs={{0,1},{1,2},{2,3},{4,5},{5,6},{6,7},{8,9},{9,10},{10,11},{12,13},{... | collective-permute-start | bytes 1572872 | tf_op jit(solution)/shard_map/ppermute | solution.py:388
  177.2 10.8 %collective-permute-start.5 = (bf16[64,16,256]{2,1,0:T(8,128)(2,1)}, bf16[64,16,256]{2,1,0:T(8,128)(2,1)}, u32[]{:S(2)}, u32[]{:S(2)}) collective-permute-start(bf16[64,16,256]{2,1,0:T(8,128)(2,1)} %copy-done.26), channel_id=1, source_target_pairs={{1,0},{2,1},{3,2},{5,4},{6,5},{7,6},{9,8},{10,9},{11,10},{13,12},{... | collective-permute-start | bytes 1572872 | tf_op jit(solution)/shard_map/ppermute | solution.py:389
  179.2 19.3 %collective-permute-start.7 = (bf16[1152,256]{1,0:T(8,128)(2,1)S(1)}, bf16[1152,256]{1,0:T(8,128)(2,1)}, u32[]{:S(2)}, u32[]{:S(2)}) collective-permute-start(bf16[1152,256]{1,0:T(8,128)(2,1)S(1)} %bitcast.22), channel_id=1, source_target_pairs={{0,1},{1,0},{2,3},{3,2},{4,5},{5,4},{6,7},{7,6},{8,9},{9,8},{10,11... | collective-permute-start | bytes 1769480 | tf_op jit(solution)/shard_map/ppermute | solution.py:431
  179.2 21.7 %collective-permute-start.9 = (bf16[1152,256]{1,0:T(8,128)(2,1)S(1)}, bf16[1152,256]{1,0:T(8,128)(2,1)S(1)}, u32[]{:S(2)}, u32[]{:S(2)}) collective-permute-start(bf16[1152,256]{1,0:T(8,128)(2,1)S(1)} %bitcast.20), channel_id=1, source_target_pairs={{0,1},{1,0},{2,3},{3,2},{4,5},{5,4},{6,7},{7,6},{8,9},{9,8},{10,11... | collective-permute-start | bytes 1769480 | tf_op jit(solution)/shard_map/ppermute | solution.py:431
  (26 other events, 48.5 us)
